TPU v7x, 512 devices: a whole 4x4x16 slice. The times are simulated.
512 devices in a mesh: grp: 16 (over z), tile: 8 (over x_hi, y), arch: 4 (over x_lo, core).
Axes of the slice: x: 4 (x_hi: 2, x_lo: 2; x = x_hi * 2 + x_lo), y: 4, z: 16, core: 2. Of those that a mesh axis runs over, the one named last changes fastest.
Arguments:
- query_grads: bfloat16 [4, 1536, 4096], P('arch', 'tile', 'grp'), may hold values from -6 to 6
- input_basis: bfloat16 [4096, 4096], P(None, 'grp'), may hold values from -0.09375 to 0.09375
- output_basis: bfloat16 [1536, 1536], P(None, 'tile'), may hold values from -0.15625 to 0.15625
- eigenvalues: float32 [1536, 4096], P('tile', 'grp'), may hold values from 0.1 to 10
- activations: bfloat16 [1024, 4096], P('arch', 'grp'), may hold values from -6 to 6
- gradients: bfloat16 [1024, 1536], P('arch', 'tile'), may hold values from -0.0099487305 to 0.0099487305
- seq_lengths: int32 [4, 8], P('arch'), may hold values from 1 to 128, 256 in all within a row
Outputs:
- preconditioned: bfloat16 [4, 4096, 1536], P('arch', 'grp', 'tile')
- sequence_scores: float32 [4, 32], P(None, 'arch')
Inputs may be any that keep to these rules, and one draw needn't show every extreme that they name: Each row of seq_lengths sums to 256, and its largest entry is exactly 128.
All inputs are finite; a program needn't handle non-finite values.
Results may differ from a plain program's by a relative error of at most 0.013.
Values may be sent and summed in bfloat16 or wider, within the bound.
A program may use at most 64 MiB of HBM per device.

v0:
```python
import jax
import jax.numpy as jnp
from jax import lax
from jax.sharding import PartitionSpec as P

damping = 0.01


def contract_first(left_side, right_side):
    return lax.dot_general(
        left_side, right_side, (((0,), (0,)), ((), ())), preferred_element_type=jnp.float32
    )


def contract_last(left_side, right_side):
    return lax.dot_general(
        left_side, right_side, (((1,), (1,)), ((), ())), preferred_element_type=jnp.float32
    )


def per_device(
    query_grads, input_basis, output_basis, eigenvalues, activations, gradients, seq_lengths
):
    local_query = query_grads[0]
    feat_rows = local_query.shape[0]
    input_cols = local_query.shape[1]
    basis_part = input_basis
    rotated_in = jnp.dot(
        lax.all_gather(local_query, "grp", axis=1, tiled=True),
        basis_part,
        preferred_element_type=jnp.float32,
    ).astype(jnp.bfloat16)
    basis_part = output_basis
    rotated = contract_first(basis_part, lax.all_gather(rotated_in, "tile", axis=0, tiled=True))
    scaled = (rotated / (eigenvalues + damping)).astype(jnp.bfloat16)
    basis_part = output_basis
    restored = lax.psum_scatter(
        jnp.dot(basis_part, scaled, preferred_element_type=jnp.float32).astype(jnp.bfloat16),
        "tile",
        scatter_dimension=0,
        tiled=True,
    )
    basis_part = input_basis
    summed = lax.psum_scatter(
        contract_last(basis_part, restored), "grp", scatter_dimension=0, tiled=True
    )
    preconditioned = summed.astype(jnp.bfloat16)
    all_queries = lax.all_gather(preconditioned[None], "arch", axis=0, tiled=True)
    query_count = all_queries.shape[0]
    stacked = jnp.transpose(all_queries, (1, 0, 2)).reshape(input_cols, query_count * feat_rows)
    projected = jnp.dot(activations, stacked, preferred_element_type=jnp.float32)
    projected = projected.reshape(activations.shape[0], query_count, feat_rows)
    partial_scores = jnp.sum(projected * gradients.astype(jnp.float32)[:, None, :], axis=2).T
    lengths = seq_lengths[0]
    ends = jnp.cumsum(lengths)
    starts = ends - lengths
    position = jnp.arange(activations.shape[0], dtype=jnp.int32)
    member = ((position[None, :] >= starts[:, None]) & (position[None, :] < ends[:, None])).astype(
        jnp.float32
    )
    seq_sizes = lengths.astype(jnp.float32)
    token_scores = lax.psum(partial_scores, ("grp", "tile"))
    totals = jnp.dot(token_scores, member.T, precision=lax.Precision.HIGHEST)
    sequence_scores = totals / seq_sizes[None, :]
    return (preconditioned[None], sequence_scores)


def solution(mesh):
    return jax.shard_map(
        per_device,
        mesh=mesh,
        in_specs=(
            P("arch", "tile", "grp"),
            P(None, "grp"),
            P(None, "tile"),
            P("tile", "grp"),
            P("arch", "grp"),
            P("arch", "tile"),
            P("arch", None),
        ),
        out_specs=(P("arch", "grp", "tile"), P(None, "arch")),
        check_vma=False,
    )
```

profile of v0, /device:TPU:2, one launch (start us, length us, event | category | flops | bytes accessed | tf_op | source)
XLA Modules:
  0.0 666.5 jit_solution(9814027762734079321)
XLA Ops:
  7.2 0.0 copy-start
  7.2 0.0 all-gather.4.cloned.1.call-start
  7.2 0.7 all-gather.4.cloned.1.call-update
  7.9 0.0 copy-start.1
  7.9 0.0 reduce-scatter.7.cloned.1.call-start
  8.0 82.4 %all-gather.4.cloned.1.call-done = bf16[1,192,4096]{2,1,0:T(8,128)(2,1)} async-done(((bf16[1,192,256]{2,1,0:T(8,128)(2,1)}), bf16[1,192,4096]{2,1,0:T(8,128)(2,1)}) %all-gather.4.cloned.1.call-update) | async-done | bytes 1572880 | tf_op jit(solution)/shard_map/all_gather | solution.py:29
  90.3 0.0 copy-done
  90.3 2.0 fusion.5
  92.3 35.8 %all_gather.10 = bf16[1536,256]{1,0:T(8,128)(2,1)S(1)} all-gather(bf16[192,256]{1,0:T(8,128)(2,1)S(1)} %fusion.5), channel_id=1, replica_groups=mesh['grp'=16,'tile'=8,'arch'=4] {'tile'}, dimensions={0}, use_global_device_ids=true | all-gather | bytes 884736 | tf_op jit(solution)/shard_map/all_gather | solution.py:34
  128.2 0.0 copy-done.1
  128.2 2.8 fusion
  131.0 2.3 copy.11
  133.3 0.0 reduce-scatter.7.cloned.1.call-update
  133.3 0.0 reduce-scatter.5.cloned.1.call-start
  133.3 81.0 %reduce-scatter.7.cloned.1.call-done = bf16[192,256]{1,0:T(8,128)(2,1)} async-done(((bf16[1536,256]{1,0:T(8,128)(2,1)}), bf16[192,256]{1,0:T(8,128)(2,1)}) %reduce-scatter.7.cloned.1.call-update) | async-done | bytes 98320
  214.3 3.4 convolution_bitcast_fusion
  217.7 0.0 copy-start.4
  217.7 0.0 copy-start.5
  217.7 0.0 copy-start.3
  217.7 0.0 reduce-scatter.5.cloned.1.call-update
  217.8 0.9 copy-done.4
  218.6 0.0 copy-done.5
  218.6 0.2 reduce-window.7
  218.8 75.6 %reduce-scatter.5.cloned.1.call-done = f32[256,192]{0,1:T(8,128)} async-done(((f32[4096,192]{0,1:T(8,128)}), f32[256,192]{0,1:T(8,128)}) %reduce-scatter.5.cloned.1.call-update) | async-done | bytes 196624 | tf_op jit(solution)/shard_map/reduce_scatter | solution.py:44
  294.4 0.0 copy-start.2
  294.4 1.0 convert_element_type.27
  295.4 6.1 all-gather.1
  301.6 0.0 copy-done.3
  301.6 0.3 fusion.15
  301.9 0.1 multiply_reduce_fusion
  302.0 356.6 %psum.7 = f32[4,256]{1,0:T(4,128)S(1)} all-reduce(f32[4,256]{1,0:T(4,128)S(1)} %bitcast.50), channel_id=1, replica_groups=mesh['grp'=16,'tile'=8,'arch'=4] {'grp','tile'}, use_global_device_ids=true, to_apply=%region_3.0 | all-reduce | flops 1024 | bytes 8192 | tf_op jit(solution)/shard_map/psum | solution.py:62
  658.6 0.8 convolution_divide_fusion
  659.4 0.0 copy-done.2
  659.4 0.7 convert_bitcast_fusion.1
  (4 shorter events, 0.0 us)
Async XLA Ops:
  7.2 83.2 %copy-start = (bf16[4096,256]{1,0:T(8,128)(2,1)S(1)}, bf16[4096,256]{1,0:T(8,128)(2,1)}, u32[]{:S(2)}) copy-start(bf16[4096,256]{1,0:T(8,128)(2,1)} %param.8) | copy-start | bytes 6291460
  7.2 83.2 %all-gather.4.cloned.1.call-start = ((), (), s32[]{:S(2)}) async-start(), calls=%async_computation.3 | async-start | bytes 1671168 | tf_op jit(solution)/shard_map/all_gather | solution.py:29
  7.9 120.3 %copy-start.1 = (bf16[1536,192]{0,1:T(8,128)(2,1)S(1)}, bf16[1536,192]{0,1:T(8,128)(2,1)}, u32[]{:S(2)}) copy-start(bf16[1536,192]{0,1:T(8,128)(2,1)} %param.9) | copy-start | bytes 1769476
  7.9 206.4 %reduce-scatter.7.cloned.1.call-start = ((), (), s32[]{:S(2)}) async-start(), calls=%async_computation.4 | async-start | bytes 884736
  133.3 161.1 %reduce-scatter.5.cloned.1.call-start = ((), (), s32[]{:S(2)}) async-start(), calls=%async_computation.2 | async-start | bytes 3342336 | tf_op jit(solution)/shard_map/reduce_scatter | solution.py:44
  217.7 0.9 copy-start.4
  217.7 0.9 copy-start.5
  217.7 83.9 %copy-start.3 = (bf16[256,256]{1,0:T(8,128)(2,1)S(1)}, bf16[256,256]{1,0:T(8,128)(2,1)}, u32[]{:S(2)}) copy-start(bf16[256,256]{1,0:T(8,128)(2,1)} %param.11) | copy-start | bytes 393220
  294.4 364.9 %copy-start.2 = (f32[256,192]{0,1:T(8,128)S(1)}, f32[256,192]{0,1:T(8,128)}, u32[]{:S(2)}) copy-start(f32[256,192]{0,1:T(8,128)} %reduce-scatter.5.cloned.1.call-done) | copy-start | bytes 589828
Sparse Core Ops, SparseCore 0:
  10.0 80.2 all-gather.3
  133.4 80.8 reduce-scatter.6
  217.9 76.5 reduce-scatter.4
where the time goes:
time: 667 us
  blocking collectives  399 us (60%)
  waiting for transfers between devices  240 us (36%)
  between operations  13.8 us (2%)
  matrix products  9.26 us (1%)
    psum x1, blocking collectives, per_device(): token_scores = lax.psum(partial_scores, ('grp', 'tile'))  357 us
    all_gather x1, waiting for transfers between devices, per_device(): lax.all_gather(local_query, 'grp', axis=1, tiled=True)  82.4 us
    unnamed x4, waiting for transfers between devices  81.7 us
    reduce_scatter x1, waiting for transfers between devices, per_device(): lax.psum_scatter(contract_last(basis_part, restored), 'grp', scatter_dime...  75.6 us
    all_gather x1, blocking collectives, per_device(): lax.all_gather(rotated_in, 'tile', axis=0, tiled=True)  35.8 us
  transfers between devices with their start and end apart: 3, of which 3 were waited for; matrix products, arithmetic and copies ran while one was open for 0% of the time, Pallas kernels for 0%

commit v1 on v0

--- a/solution.py
+++ b/solution.py
@@ -59,7 +59,7 @@
         jnp.float32
     )
     seq_sizes = lengths.astype(jnp.float32)
-    token_scores = lax.psum(partial_scores, ("grp", "tile"))
+    token_scores = lax.psum(lax.psum(partial_scores, "grp"), "tile")
     totals = jnp.dot(token_scores, member.T, precision=lax.Precision.HIGHEST)
     sequence_scores = totals / seq_sizes[None, :]
     return (preconditioned[None], sequence_scores)

time: 667 us -> 362 us (0.54)
  the two profiles are of different devices: /device:TPU:2 before, /device:TPU:32 now
where the time goes in v1:
time: 362 us
  waiting for transfers between devices  238 us (66%)
  blocking collectives  94.8 us (26%)
  between operations  13.8 us (4%)
  matrix products  9.28 us (3%)
    unnamed x4, waiting for transfers between devices  82.5 us
    all_gather x1, waiting for transfers between devices, per_device(): lax.all_gather(local_query, 'grp', axis=1, tiled=True)  81.7 us
    reduce_scatter x1, waiting for transfers between devices, per_device(): lax.psum_scatter(contract_last(basis_part, restored), 'grp', scatter_dime...  74.2 us
    psum x2, blocking collectives, per_device(): token_scores = lax.psum(lax.psum(partial_scores, 'grp'), 'tile')  52.1 us
    all_gather x1, blocking collectives, per_device(): lax.all_gather(rotated_in, 'tile', axis=0, tiled=True)  36 us
  transfers between devices with their start and end apart: 3, of which 3 were waited for; matrix products, arithmetic and copies ran while one was open for 0% of the time, Pallas kernels for 0%

profile of v1, /device:TPU:32, one launch (start us, length us, event | category | flops | bytes accessed | tf_op | source)
XLA Modules:
  0.0 361.5 jit_solution(17599551943291472414)
XLA Ops:
  7.2 0.0 copy-start
  7.2 0.0 all-gather.4.cloned.1.call-start
  7.2 0.7 all-gather.4.cloned.1.call-update
  7.9 0.0 copy-start.1
  7.9 0.0 reduce-scatter.7.cloned.1.call-start
  8.0 81.7 %all-gather.4.cloned.1.call-done = bf16[1,192,4096]{2,1,0:T(8,128)(2,1)} async-done(((bf16[1,192,256]{2,1,0:T(8,128)(2,1)}), bf16[1,192,4096]{2,1,0:T(8,128)(2,1)}) %all-gather.4.cloned.1.call-update) | async-done | bytes 1572880 | tf_op jit(solution)/shard_map/all_gather | solution.py:29
  89.7 0.0 copy-done
  89.7 2.0 fusion.5
  91.7 36.0 %all_gather.10 = bf16[1536,256]{1,0:T(8,128)(2,1)S(1)} all-gather(bf16[192,256]{1,0:T(8,128)(2,1)S(1)} %fusion.5), channel_id=1, replica_groups=mesh['grp'=16,'tile'=8,'arch'=4] {'tile'}, dimensions={0}, use_global_device_ids=true | all-gather | bytes 884736 | tf_op jit(solution)/shard_map/all_gather | solution.py:34
  127.7 0.0 copy-done.1
  127.7 2.8 fusion
  130.5 2.3 copy.11
  132.8 0.0 reduce-scatter.7.cloned.1.call-update
  132.8 0.0 reduce-scatter.5.cloned.1.call-start
  132.9 81.8 %reduce-scatter.7.cloned.1.call-done = bf16[192,256]{1,0:T(8,128)(2,1)} async-done(((bf16[1536,256]{1,0:T(8,128)(2,1)}), bf16[192,256]{1,0:T(8,128)(2,1)}) %reduce-scatter.7.cloned.1.call-update) | async-done | bytes 98320
  214.7 3.4 convolution_bitcast_fusion
  218.1 0.0 copy-start.4
  218.1 0.0 copy-start.5
  218.1 0.0 copy-start.3
  218.1 0.0 reduce-scatter.5.cloned.1.call-update
  218.1 0.9 copy-done.4
  219.0 0.0 copy-done.5
  219.0 0.2 reduce-window.7
  219.2 74.2 %reduce-scatter.5.cloned.1.call-done = f32[256,192]{0,1:T(8,128)} async-done(((f32[4096,192]{0,1:T(8,128)}), f32[256,192]{0,1:T(8,128)}) %reduce-scatter.5.cloned.1.call-update) | async-done | bytes 196624 | tf_op jit(solution)/shard_map/reduce_scatter | solution.py:44
  293.4 0.0 copy-start.2
  293.4 1.0 convert_element_type.27
  294.4 6.7 %all-gather.1 = bf16[1024,192]{0,1:T(8,128)(2,1)S(1)} all-gather(bf16[256,192]{0,1:T(8,128)(2,1)S(1)} %convert_element_type.27), channel_id=3, replica_groups=mesh['grp'=16,'tile'=8,'arch'=4] {'arch'}, dimensions={0}, use_global_device_ids=true | all-gather | bytes 491520 | tf_op jit(solution)/shard_map/all_gather | solution.py:48
  301.1 0.0 copy-done.3
  301.1 0.3 fusion.15
  301.4 0.1 multiply_reduce_fusion
  301.5 28.0 %psum.14 = f32[4,256]{1,0:T(4,128)S(1)} all-reduce(f32[4,256]{1,0:T(4,128)S(1)} %bitcast.50), channel_id=1, replica_groups=mesh['grp'=16,'tile'=8,'arch'=4] {'grp'}, use_global_device_ids=true, to_apply=%region_3.0 | all-reduce | flops 1024 | bytes 8192 | tf_op jit(solution)/shard_map/psum | solution.py:62
  329.5 24.1 %psum.15 = f32[4,256]{1,0:T(4,128)S(1)} all-reduce(f32[4,256]{1,0:T(4,128)S(1)} %psum.14), channel_id=1, replica_groups=mesh['grp'=16,'tile'=8,'arch'=4] {'tile'}, use_global_device_ids=true, to_apply=%region_4.5 | all-reduce | flops 1024 | bytes 8192 | tf_op jit(solution)/shard_map/psum | solution.py:62
  353.6 0.8 convolution_divide_fusion
  354.3 0.0 copy-done.2
  354.4 0.7 convert_bitcast_fusion.1
  (4 shorter events, 0.0 us)
Async XLA Ops:
  7.2 82.5 %copy-start = (bf16[4096,256]{1,0:T(8,128)(2,1)S(1)}, bf16[4096,256]{1,0:T(8,128)(2,1)}, u32[]{:S(2)}) copy-start(bf16[4096,256]{1,0:T(8,128)(2,1)} %param.8) | copy-start | bytes 6291460
  7.2 82.5 %all-gather.4.cloned.1.call-start = ((), (), s32[]{:S(2)}) async-start(), calls=%async_computation.3 | async-start | bytes 1671168 | tf_op jit(solution)/shard_map/all_gather | solution.py:29
  7.9 119.8 %copy-start.1 = (bf16[1536,192]{0,1:T(8,128)(2,1)S(1)}, bf16[1536,192]{0,1:T(8,128)(2,1)}, u32[]{:S(2)}) copy-start(bf16[1536,192]{0,1:T(8,128)(2,1)} %param.9) | copy-start | bytes 1769476
  7.9 206.8 %reduce-scatter.7.cloned.1.call-start = ((), (), s32[]{:S(2)}) async-start(), calls=%async_computation.4 | async-start | bytes 884736
  132.8 160.5 %reduce-scatter.5.cloned.1.call-start = ((), (), s32[]{:S(2)}) async-start(), calls=%async_computation.2 | async-start | bytes 3342336 | tf_op jit(solution)/shard_map/reduce_scatter | solution.py:44
  218.1 0.9 copy-start.4
  218.1 0.9 copy-start.5
  218.1 83.0 %copy-start.3 = (bf16[256,256]{1,0:T(8,128)(2,1)S(1)}, bf16[256,256]{1,0:T(8,128)(2,1)}, u32[]{:S(2)}) copy-start(bf16[256,256]{1,0:T(8,128)(2,1)} %param.11) | copy-start | bytes 393220
  293.4 61.0 %copy-start.2 = (f32[256,192]{0,1:T(8,128)S(1)}, f32[256,192]{0,1:T(8,128)}, u32[]{:S(2)}) copy-start(f32[256,192]{0,1:T(8,128)} %reduce-scatter.5.cloned.1.call-done) | copy-start | bytes 589828
Sparse Core Ops, SparseCore 0:
  10.0 79.6 all-gather.3
  133.0 81.6 reduce-scatter.6
  218.2 75.1 reduce-scatter.4
